TPU v7x, 128 devices: a whole 4x4x4 slice. The times are simulated.
128 devices in a mesh: pts: 8 (over z, x_hi), lmk: 16 (over y, x_lo, core).
Axes of the slice: x: 4 (x_hi: 2, x_lo: 2; x = x_hi * 2 + x_lo), y: 4, z: 4, core: 2. Of those that a mesh axis runs over, the one named last changes fastest.
Arguments:
- points: bfloat16 [262144, 128], P('pts'), may hold values from -3.5 to 3.5
- landmark_ids: int32 [16384], P('lmk'), may hold values from 0 to 262143, as said below
- coefficients: bfloat16 [16384, 32], P('lmk'), may hold values from -192 to 192
Outputs:
- product: float32 [16384, 32], P(('lmk', 'pts'))
Inputs may be any that keep to these rules, and one draw needn't show every extreme that they name: `landmark_ids`: landmarks fall unevenly on the point blocks of 32768 rows; indices may repeat; 0 and 262143 occur in every draw.
All inputs are finite; a program needn't handle non-finite values.
Results may differ from a plain program's by a relative error of at most 0.00045.
Values may be sent and summed in bfloat16 or wider, within the bound.
A program may use at most 128 MiB of HBM per device.

v0:
```python
import jax
import jax.numpy as jnp
from jax import lax
from jax.sharding import PartitionSpec as P

BLOCK = 2048


GAMMA = 0.25


def kernel_tile(rows, centers, center_sq):
    cross = jnp.dot(rows, centers.T, preferred_element_type=jnp.float32)
    row_f = rows.astype(jnp.float32)
    row_sq = jnp.sum(row_f * row_f, axis=1)
    dist = row_sq[:, None] + center_sq[None, :] - 2.0 * cross
    return jnp.exp(-GAMMA * dist).astype(jnp.bfloat16)


def transposed(tile, fitted):
    return lax.dot_general(
        tile, fitted, (((0,), (0,)), ((), ())), preferred_element_type=jnp.float32
    )


def per_device(points, landmark_ids, coefficients):
    pts_rows = points.shape[0]
    width = points.shape[1]
    outs_count = coefficients.shape[1]
    here = lax.axis_index("pts")
    local_ids = landmark_ids - here * pts_rows
    owned = (local_ids >= 0) & (local_ids < pts_rows)
    picked = jnp.take(points, jnp.clip(local_ids, 0, pts_rows - 1), axis=0).astype(jnp.float32)
    picked = jnp.where(owned[:, None], picked, 0.0)
    centers = lax.psum(picked.astype(jnp.bfloat16), "pts")
    center_f = centers.astype(jnp.float32)
    center_sq = jnp.sum(center_f * center_f, axis=1)
    blocks = points.reshape(pts_rows // BLOCK, BLOCK, width)
    start = jnp.zeros((centers.shape[0], outs_count), jnp.float32)

    def fit_block(rows):
        tile = kernel_tile(rows, centers, center_sq)
        return jnp.dot(tile, coefficients, preferred_element_type=jnp.float32)

    partial_fit = lax.map(fit_block, blocks)
    fitted = lax.psum(partial_fit.astype(jnp.bfloat16), "lmk")

    def back_step(total, pair):
        rows, fitted_rows = pair
        tile = kernel_tile(rows, centers, center_sq)
        return (total + transposed(tile, fitted_rows), None)

    total, unused = lax.scan(back_step, start, (blocks, fitted))
    summed = lax.psum_scatter(total, "pts", scatter_dimension=0, tiled=True)
    return summed / (pts_rows * lax.axis_size("pts"))


def solution(mesh):
    placed = (P("pts", None), P("lmk"), P("lmk", None))
    return jax.shard_map(
        per_device, mesh=mesh, in_specs=placed, out_specs=P(("lmk", "pts"), None), check_vma=False
    )
```

profile of v0, /device:TPU:1, one launch (start us, length us, event | category | flops | bytes accessed | tf_op | source)
XLA Modules:
  0.0 479.3 jit_solution(15810703086927467805)
XLA Ops:
  7.9 7.3 %gather_fusion = bf16[1024,128]{1,0:T(8,128)(2,1)S(1)} fusion(bf16[32768,128]{1,0:T(8,128)(2,1)} %param.7, s32[1024]{0:T(1024)S(1)} %fusion.21), kind=kCustom, calls=%fused_computation | custom fusion | bytes 528384 | tf_op jit(solution)/shard_map/jit(_take)/gather | solution.py:33
  16.4 82.7 %all-reduce.3.cloned.1.call-done = bf16[1024,128]{1,0:T(8,128)(2,1)} async-done(((bf16[1024,128]{1,0:T(8,128)(2,1)}), bf16[1024,128]{1,0:T(8,128)(2,1)}) %all-reduce.3.cloned.1.call-update) | async-done | bytes 262160 | tf_op jit(solution)/shard_map/psum | solution.py:35
  100.2 95.3 %while.21 = (s32[]{:T(128)}, bf16[16,2048,32]{1,2,0:T(8,128)(2,1)}, bf16[16,2048,128]{2,1,0:T(8,128)(2,1)}, f32[1024]{0:T(1024)S(1)}, bf16[1024,128]{1,0:T(8,128)(2,1)}, /*index=5*/bf16[1024,32]{0,1:T(8,128)(2,1)}, s32[]{:T(128)}) while((s32[]{:T(128)}, bf16[16,2048,32]{1,2,0:T(8,128)(2,1)}, bf16[16,2048,128]{2,1,0:T(8,128)(2,1)}, ...), condition=%wide.region_4.5_spmd, body=%wide.region_2.4_spmd.sunk | while | flops 682358784 | bytes 1659985 | solution.py:45
  101.7 4.6 fusion.36
  107.6 4.6 fusion.36
  113.6 4.6 fusion.36
  119.5 4.6 fusion.36
  125.5 4.5 fusion.36
  131.4 4.6 fusion.36
  137.4 4.6 fusion.36
  143.3 4.6 fusion.36
  149.3 4.6 fusion.36
  155.2 4.6 fusion.36
  161.2 4.6 fusion.36
  167.1 4.6 fusion.36
  173.1 4.5 fusion.36
  179.0 4.6 fusion.36
  185.0 4.6 fusion.36
  190.9 4.6 fusion.36
  195.6 127.1 %all-reduce.5.cloned.1.call-done = bf16[16,2048,32]{1,2,0:T(8,128)(2,1)} async-done(((bf16[16,2048,32]{1,2,0:T(8,128)(2,1)}), bf16[16,2048,32]{1,2,0:T(8,128)(2,1)}) %all-reduce.5.cloned.1.call-update) | async-done | bytes 2097168 | tf_op jit(solution)/shard_map/psum | solution.py:46
  322.7 79.2 %while.22 = (s32[]{:T(128)}, f32[1024,32]{0,1:T(8,128)S(1)}, bf16[16,2048,128]{2,1,0:T(8,128)(2,1)}, f32[1024]{0:T(1024)S(1)}, bf16[1024,128]{1,0:T(8,128)(2,1)}...) while((s32[]{:T(128)}, f32[1024,32]{0,1:T(8,128)S(1)}, ...), condition=%wide.region_8.9_spmd.clone, body=%wide.region_6.8_spmd.clone.sunk | while | flops 682424320 | bytes 1725539 | solution.py:53
  353.8 3.5 fusion.40
  358.7 3.5 fusion.40
  363.7 3.5 fusion.40
  368.6 3.5 fusion.40
  373.6 3.5 fusion.40
  378.5 3.5 fusion.40
  383.5 3.5 fusion.40
  388.4 3.5 fusion.40
  393.4 3.5 fusion.40
  398.3 3.5 fusion.40
  402.5 68.9 %reduce-scatter.2.cloned.1.call-done = f32[128,32]{0,1:T(8,128)} async-done(((f32[1024,32]{0,1:T(8,128)}), f32[128,32]{0,1:T(8,128)}) %reduce-scatter.2.cloned.1.call-update) | async-done | bytes 16400 | tf_op jit(solution)/shard_map/reduce_scatter | solution.py:54
  (53 shorter events, 71.2 us)
Async XLA Ops:
  6.5 92.5 %all-reduce.3.cloned.1.call-start = ((), (), s32[]{:S(2)}) async-start(), calls=%async_computation.1 | async-start | bytes 524288 | tf_op jit(solution)/shard_map/psum | solution.py:35
  16.3 306.3 %all-reduce.5.cloned.1.call-start = ((), (), s32[]{:S(2)}) async-start(), calls=%async_computation.2 | async-start | bytes 4194304 | tf_op jit(solution)/shard_map/psum | solution.py:46
  195.5 275.9 %reduce-scatter.2.cloned.1.call-start = ((), (), s32[]{:S(2)}) async-start(), calls=%async_computation.3 | async-start | bytes 147456 | tf_op jit(solution)/shard_map/reduce_scatter | solution.py:54
  401.9 0.6 copy-start
Sparse Core Ops, SparseCore 0:
  16.5 82.5 all-reduce.2
  195.6 126.9 all-reduce.4
  402.7 68.7 reduce-scatter.1
where the time goes:
time: 483 us; the launch traced here: 479 us
  waiting for transfers between devices  279 us (58%)
  matrix products  129 us (27%)
  other arithmetic  49.2 us (10%)
  between operations  13.2 us (3%)
  local copies, waits for them, and re-layouts  7.97 us (2%)
    psum x1, waiting for transfers between devices, per_device(): fitted = lax.psum(partial_fit.astype(jnp.bfloat16), 'lmk')  127 us
    psum x1, waiting for transfers between devices, per_device(): centers = lax.psum(picked.astype(jnp.bfloat16), 'pts')  82.7 us
    dot_general x16, matrix products, fit_block(): return jnp.dot(tile, coefficients, preferred_element_type=jnp.float32)  73 us
    reduce_scatter x1, waiting for transfers between devices, per_device(): summed = lax.psum_scatter(total, 'pts', scatter_dimension=0, tiled=True)  68.9 us
    dot_general x16, matrix products, transposed(): lax.dot_general(tile, fitted, (((0,), (0,)), ((), ())), preferred_element...  56.5 us
    reduce_sum x32, other arithmetic, kernel_tile(): row_sq = jnp.sum(row_f * row_f, axis=1)  44.3 us
  transfers between devices with their start and end apart: 3, of which 3 were waited for; matrix products, arithmetic and copies ran while one was open for 0% of the time, Pallas kernels for 0%

commit v1 on v0

v1 whole, which is shorter than its diff:
```python
import functools

import jax
import jax.numpy as jnp
from jax import lax
from jax.experimental import pallas as pl
from jax.experimental.pallas import tpu as pltpu
from jax.sharding import PartitionSpec as P

MESH = pl.DeviceIdType.MESH
BF16, F32 = jnp.bfloat16, jnp.float32
GROUPS = 8
CHUNK = 1024
STEP = 4096
PIECES = 2 * GROUPS
PIECE = STEP // PIECES
SLOTS = 4
NT = (((1,), (1,)), ((), ()))


def dot(a, b, dims=(((1,), (0,)), ((), ()))):
    return lax.dot_general(a, b, dims, preferred_element_type=F32)


def augment(rows_f):
    sq = -0.25 * jnp.sum(rows_f * rows_f, axis=1, keepdims=True)
    hi = sq.astype(BF16).astype(F32)
    mid = (sq - hi).astype(BF16).astype(F32)
    low = sq - hi - mid
    lane = lax.broadcasted_iota(jnp.int32, rows_f.shape, 1)
    return jnp.where(lane == 0, hi, jnp.where(lane == 1, mid, jnp.where(lane == 2, low, 0.0))).astype(BF16)


def square_row(rows):
    rows_f = rows.astype(F32)
    squares = rows_f * rows_f
    hi = squares.astype(BF16)
    low = (squares - hi.astype(F32)).astype(BF16)
    quarter = jnp.full((8, 2 * rows.shape[1]), -0.25, BF16)
    return dot(quarter, jnp.concatenate([hi, low], axis=1), NT)[:1]


def body(steps, picked, coef_t, points, out, xm, sq, ca, rows_in, centers, kt, part, p1r, p2s, p2r, fit, prod, prod_t,
         prod_in, load_sem, c_send, c_recv, s1, r1, s2, r2, s3, r3, s4, r4, o_send, o_recv):
    here = lax.axis_index("pts")
    lmk = lax.axis_index("lmk")
    chip, core = lmk // 2, lmk % 2
    other = chip * 2 + 1 - core

    def load(i):
        rows = pl.ds(i * STEP, STEP)
        return pltpu.make_async_copy(points.at[rows], xm.at[rows], load_sem.at[i])

    def start_load(i, carry):
        load(i).start()
        return carry

    lax.fori_loop(0, steps, start_load, 0)

    barrier = pltpu.get_barrier_semaphore()
    for k in range(GROUPS - 1):
        pl.semaphore_signal(barrier, inc=1, device_id={"pts": (here + k + 1) % GROUPS}, device_id_type=MESH)
        pl.semaphore_signal(barrier, inc=1, device_id={"lmk": ((chip + k + 1) % GROUPS) * 2 + core}, device_id_type=MESH)
    pl.semaphore_signal(barrier, inc=1, device_id={"lmk": other}, device_id_type=MESH)
    pl.semaphore_wait(barrier, 2 * GROUPS - 1)

    def along_pts(src, dst, send, recv, peer):
        return pltpu.make_async_remote_copy(src, dst, send, recv, device_id={"pts": peer}, device_id_type=MESH)

    def along_lmk(src, dst, send, recv, peer):
        return pltpu.make_async_remote_copy(src, dst, send, recv, device_id={"lmk": peer}, device_id_type=MESH)

    for k in range(GROUPS - 1):
        peer = (here + k + 1) % GROUPS
        along_pts(picked.at[peer], rows_in.at[k], c_send.at[0], c_recv.at[0], peer).start()

    def prepare(i, carry):
        load(i).wait()
        for h in range(STEP // CHUNK):
            rows = pl.ds(i * STEP + h * CHUNK, CHUNK)
            sq[i, :, pl.ds(h * CHUNK, CHUNK)] = square_row(xm[rows, :])
        return carry

    lax.fori_loop(0, steps // 2, prepare, 0)
    along_pts(rows_in, rows_in, c_send.at[0], c_recv.at[0], here).wait_recv()
    total = picked[here].astype(F32)
    for k in range(GROUPS - 1):
        total = total + rows_in[k].astype(F32)
    centers[here] = total.astype(BF16)
    for k in range(GROUPS - 1):
        peer = (here + k + 1) % GROUPS
        along_pts(centers.at[here], centers.at[here], c_send.at[1], c_recv.at[1], peer).start()
    lax.fori_loop(steps // 2, steps, prepare, 0)
    along_pts(rows_in, rows_in, c_send.at[1], c_recv.at[1], here).wait_recv()
    for g in range(GROUPS):
        rows_f = centers[g].astype(F32)
        ca[pl.ds(g * 128, 128), pl.ds(0, 128)] = (0.5 * rows_f).astype(BF16)
        ca[pl.ds(g * 128, 128), pl.ds(128, 128)] = augment(rows_f)
    prod[...] = jnp.zeros_like(prod)

    def copy1(b):
        return along_lmk(part.at[b, pl.ds((1 - core) * GROUPS, GROUPS)], p1r.at[b], s1.at[b], r1.at[b], other)

    def copy4(b):
        half = fit.at[b, pl.ds(core * GROUPS, GROUPS)]
        return along_lmk(half, half, s4.at[b], r4.at[b], other)

    def all2(b):
        return along_lmk(p2r.at[b], p2r.at[b], s2.at[b], r2.at[b], other)

    def all3(b):
        return along_lmk(p2r.at[b], p2r.at[b], s3.at[b], r3.at[b], other)

    lane = lax.broadcasted_iota(jnp.int32, (CHUNK, 128), 1)
    ones = jnp.where(lane < 3, 1.0, 0.0).astype(BF16)

    def step(t, carry):
        @pl.when(t >= SLOTS)
        def _():
            b = t - SLOTS
            copy4(b).wait_recv()
            fitted_t = jnp.concatenate([fit[b, q] for q in range(PIECES)], axis=1)
            prod[...] += dot(kt[b % SLOTS], fitted_t, NT)

        @pl.when(t < steps)
        def _():
            def tiles(h, carry):
                at = pl.multiple_of(t * STEP + h * CHUNK, CHUNK)
                rows = jnp.concatenate([xm[pl.ds(at, CHUNK), :], ones], axis=1)
                sq_row = sq[t, :, pl.ds(pl.multiple_of(h * CHUNK, CHUNK), CHUNK)]
                tile = jnp.exp(dot(ca[...], rows, NT) + sq_row).astype(BF16)
                kt[t % SLOTS, :, pl.ds(pl.multiple_of(h * CHUNK, CHUNK), CHUNK)] = tile
                partial_t = dot(coef_t[...], tile).astype(BF16)
                for q in range(CHUNK // PIECE):
                    part[t, h * (CHUNK // PIECE) + q] = partial_t[:, q * PIECE : (q + 1) * PIECE]
                return carry

            lax.fori_loop(0, STEP // CHUNK, tiles, 0)
            copy1(t).start()

        @pl.when((t >= 1) & (t < steps + 1))
        def _():
            b = t - 1
            copy1(b).wait_recv()
            for g in range(GROUPS):
                p2s[b, g] = (part[b, core * GROUPS + g].astype(F32) + p1r[b, g].astype(F32)).astype(BF16)
            for k in range(GROUPS - 1):
                peer = (chip + k + 1) % GROUPS
                along_lmk(p2s.at[b, peer], p2r.at[b, k], s2.at[b], r2.at[b], peer * 2 + core).start()

        @pl.when((t >= 2) & (t < steps + 2))
        def _():
            b = t - 2
            all2(b).wait_recv()
            total = p2s[b, chip].astype(F32)
            for k in range(GROUPS - 1):
                total = total + p2r[b, k].astype(F32)
            mine = core * GROUPS + chip
            fit[b, mine] = total.astype(BF16)
            for k in range(GROUPS - 1):
                peer = (chip + k + 1) % GROUPS
                along_lmk(fit.at[b, mine], fit.at[b, mine], s3.at[b], r3.at[b], peer * 2 + core).start()

        @pl.when((t >= 3) & (t < steps + 3))
        def _():
            b = t - 3
            all3(b).wait_recv()
            copy4(b).start()

        return carry

    lax.fori_loop(0, steps + SLOTS, step, 0)

    for g in range(GROUPS):
        prod_t[g] = prod[pl.ds(g * 128, 128), :].T
    for k in range(GROUPS - 1):
        peer = (here + k + 1) % GROUPS
        along_pts(prod_t.at[peer], prod_in.at[k], o_send, o_recv, peer).start()

    def sent(b, carry):
        copy1(b).wait_send()
        all2(b).wait_send()
        all3(b).wait_send()
        copy4(b).wait_send()
        return carry

    lax.fori_loop(0, steps, sent, 0)
    for i in range(2):
        along_pts(rows_in, rows_in, c_send.at[i], c_recv.at[i], here).wait_send()
    along_pts(prod_in, prod_in, o_send, o_recv, here).wait_recv()
    total = prod_t[here]
    for k in range(GROUPS - 1):
        total = total + prod_in[k]
    out[...] = total.T * (1.0 / (steps * STEP * GROUPS))
    along_pts(prod_in, prod_in, o_send, o_recv, here).wait_send()


def per_device(points, landmark_ids, coefficients):
    pts_rows, width = points.shape
    marks, outs_count = coefficients.shape
    steps = pts_rows // STEP
    here = lax.axis_index("pts")
    local_ids = landmark_ids - here * pts_rows
    owned = (local_ids >= 0) & (local_ids < pts_rows)
    picked = jnp.take(points, jnp.clip(local_ids, 0, pts_rows - 1), axis=0)
    picked = jnp.where(owned[:, None], picked, jnp.zeros((), BF16)).reshape(GROUPS, marks // GROUPS, width)
    vmem = pl.BlockSpec(memory_space=pltpu.VMEM)
    dma = pltpu.SemaphoreType.DMA
    return pl.pallas_call(
        functools.partial(body, steps),
        out_shape=jax.ShapeDtypeStruct((marks // GROUPS, outs_count), F32),
        in_specs=[vmem, vmem, pl.BlockSpec(memory_space=pl.ANY)],
        out_specs=vmem,
        scratch_shapes=[
            pltpu.VMEM((pts_rows, width), BF16),
            pltpu.VMEM((steps, 1, STEP), F32),
            pltpu.VMEM((marks, width + 128), BF16),
            pltpu.VMEM((GROUPS - 1, marks // GROUPS, width), BF16),
            pltpu.VMEM((GROUPS, marks // GROUPS, width), BF16),
            pltpu.VMEM((SLOTS, marks, STEP), BF16),
            pltpu.VMEM((steps, PIECES, outs_count, PIECE), BF16),
            pltpu.VMEM((steps, GROUPS, outs_count, PIECE), BF16),
            pltpu.VMEM((steps, GROUPS, outs_count, PIECE), BF16),
            pltpu.VMEM((steps, GROUPS - 1, outs_count, PIECE), BF16),
            pltpu.VMEM((steps, PIECES, outs_count, PIECE), BF16),
            pltpu.VMEM((marks, outs_count), F32),
            pltpu.VMEM((GROUPS, outs_count, 128), F32),
            pltpu.VMEM((GROUPS - 1, outs_count, 128), F32),
            dma((steps,)),
            dma((2,)),
            dma((2,)),
        ]
        + [dma((steps,))] * 8
        + [dma(()), dma(())],
        compiler_params=pltpu.CompilerParams(collective_id=0, has_side_effects=True, vmem_limit_bytes=60 * 2**20),
    )(picked, coefficients.T, points)


def solution(mesh):
    placed = (P("pts", None), P("lmk"), P("lmk", None))
    return jax.shard_map(
        per_device, mesh=mesh, in_specs=placed, out_specs=P(("lmk", "pts"), None), check_vma=False
    )
```

time: 483 us -> 104 us (0.22)
  waiting for transfers between devices: 279 us -> 0 us
  matrix products: 129 us -> 0 us
  Pallas kernels: 0 us -> 92.3 us
  other arithmetic: 49.2 us -> 2.43 us
  between operations: 13.2 us -> 0.02 us
    psum x2 -> x0, waiting for transfers between devices: 210 us -> none  [the longest x1 127 us: per_device(): fitted = lax.psum(partial_fit.astype(jnp.bfloat16), 'lmk')]
    dot_general x32 -> x0, matrix products: 129 us -> none  [the longest x16 73 us: fit_block(): return jnp.dot(tile, coefficients, preferred_element_type=jnp.float32)]
    pallas_call x0 -> x1, Pallas kernels: none -> 92.3 us  [per_device(): pl.pallas_call(functools.partial(body, steps), out_shape=jax.ShapeDtypeSt...]
    reduce_scatter x1 -> x0, waiting for transfers between devices: 68.9 us -> none  [per_device(): summed = lax.psum_scatter(total, 'pts', scatter_dimension=0, tiled=True)]
    reduce_sum x33 -> x0, other arithmetic: 45.5 us -> none  [the longest x32 44.3 us: kernel_tile(): row_sq = jnp.sum(row_f * row_f, axis=1)]
  transfers between devices with their start and end apart: 3 -> 0, of which waited for: 3 -> 0; matrix products, arithmetic and copies ran while one was open for 0% -> 0% of each run, Pallas kernels for 0% -> 0%
where the time goes in v1:
time: 104 us
  Pallas kernels  92.3 us (89%)
  local copies, waits for them, and re-layouts  8.85 us (9%)
  other arithmetic  2.43 us (2%)
    pallas_call x1, Pallas kernels, per_device(): pl.pallas_call(functools.partial(body, steps), out_shape=jax.ShapeDtypeSt...  92.3 us
    gather x1, local copies, waits for them, and re-layouts, per_device(): picked = jnp.take(points, jnp.clip(local_ids, 0, pts_rows - 1), axis=0)  7.33 us

profile of v1, /device:TPU:1, one launch (start us, length us, event | category | flops | bytes accessed | tf_op | source)
XLA Modules:
  0.0 103.6 jit_solution(7885037159763824677)
XLA Ops:
  0.0 0.7 and_bitcast_fusion.1
  0.7 0.7 fusion
  1.4 7.3 %gather_fusion = bf16[1024,128]{1,0:T(8,128)(2,1)S(1)} fusion(bf16[32768,128]{1,0:T(8,128)(2,1)} %points.1, s32[1024]{0:T(1024)S(1)} %fusion), kind=kCustom, calls=%fused_computation | custom fusion | bytes 528384 | tf_op jit(solution)/shard_map/jit(_take)/gather | solution.py:205
  8.7 1.0 select_select_fusion.picked
  9.8 92.3 %shard_map.37 = f32[128,32]{1,0:T(8,128)} custom-call(bf16[8,128,128]{2,1,0:T(8,128)(2,1)} %select_select_fusion.picked, bf16[32,1024]{1,0:T(8,128)(2,1)} %bitcast.7, bf16[32768,128]{1,0:T(8,128)(2,1)} %points.1), custom_call_target="tpu_custom_call" | custom-call | tf_op jit(solution)/shard_map/pallas_call | solution.py:209
  102.1 1.5 %copy.4 = f32[128,32]{0,1:T(8,128)} copy(f32[128,32]{1,0:T(8,128)} %shard_map.37) | data formatting | bytes 32768 | tf_op jit(solution)/shard_map/pallas_call | solution.py:209

commit v2 on v1

v2 whole, which is shorter than its diff:
```python
import functools

import jax
import jax.numpy as jnp
from jax import lax
from jax.experimental import pallas as pl
from jax.experimental.pallas import tpu as pltpu
from jax.sharding import PartitionSpec as P

MESH = pl.DeviceIdType.MESH
BF16, F32 = jnp.bfloat16, jnp.float32
GROUPS = 8
TILE = 256
UNITS = 8
PIECES = 2 * UNITS
STEP = PIECES * TILE
SLOTS = 4
LAG = 3
SEG, RING = 128, 3
MXUS = (0, 1)


def augment(rows_f):
    sq = -0.25 * jnp.sum(rows_f * rows_f, axis=1, keepdims=True)
    hi = sq.astype(BF16).astype(F32)
    mid = (sq - hi).astype(BF16).astype(F32)
    low = sq - hi - mid
    lane = lax.broadcasted_iota(jnp.int32, rows_f.shape, 1)
    return jnp.where(lane == 0, hi, jnp.where(lane == 1, mid, jnp.where(lane == 2, low, 0.0))).astype(BF16)


def halves(rows):
    rows_f = rows.astype(F32)
    squares = rows_f * rows_f
    hi = squares.astype(BF16)
    return jnp.concatenate([hi, (squares - hi.astype(F32)).astype(BF16)], axis=1)


def body(steps, ids, coef, points, out, xm, sq, ca, ct, picked_f, picked, rows_in, centers, pb0, pb1, part, p1r, p2s, p2r,
         fit, prod_t, prod_in, load_sem, c_send, c_recv, s1, r1, s2, r2, s3, r3, s4, r4, o_send, o_recv):
    here = lax.axis_index("pts")
    lmk = lax.axis_index("lmk")
    chip, core = lmk // 2, lmk % 2
    other = chip * 2 + 1 - core
    slab, width = xm.shape
    marks = coef.shape[0]
    outs = coef.shape[1]
    pb = (pb0, pb1)

    def load(i):
        rows = pl.ds(i * STEP, STEP)
        return pltpu.make_async_copy(points.at[rows], xm.at[rows], load_sem.at[i])

    def start_load(i, carry):
        load(i).start()
        return carry

    lax.fori_loop(0, steps, start_load, 0)

    barrier = pltpu.get_barrier_semaphore()
    for k in range(GROUPS - 1):
        pl.semaphore_signal(barrier, inc=1, device_id={"pts": (here + k + 1) % GROUPS}, device_id_type=MESH)
        pl.semaphore_signal(barrier, inc=1, device_id={"lmk": ((chip + k + 1) % GROUPS) * 2 + core}, device_id_type=MESH)
    pl.semaphore_signal(barrier, inc=1, device_id={"lmk": other}, device_id_type=MESH)

    def gather(xf):
        def widen(i, carry):
            load(i).wait()
            for h in range(8):
                rows = pl.ds(i * STEP + h * (STEP // 8), STEP // 8)
                xf[rows, :] = xm[rows, :].astype(F32)
            return carry

        lax.fori_loop(0, steps, widen, 0)

        def pick(i, carry):
            first = pl.multiple_of(i * 32, 32)
            for u in range(32):
                at = ids[first + u] - here * slab
                row = xf[pl.ds(jnp.clip(at, 0, slab - 1), 1), :]
                picked_f[pl.ds(first + u, 1), :] = jnp.where((at >= 0) & (at < slab), row, 0.0)
            return carry

        lax.fori_loop(0, marks // 32, pick, 0)

    pl.run_scoped(gather, pltpu.VMEM((slab, width), F32))
    for g in range(GROUPS):
        picked[g] = picked_f[pl.ds(g * 128, 128), :].astype(BF16)
    pl.semaphore_wait(barrier, 2 * GROUPS - 1)

    def along_pts(src, dst, send, recv, peer):
        return pltpu.make_async_remote_copy(src, dst, send, recv, device_id={"pts": peer}, device_id_type=MESH)

    def along_lmk(src, dst, send, recv, peer):
        return pltpu.make_async_remote_copy(src, dst, send, recv, device_id={"lmk": peer}, device_id_type=MESH)

    for k in range(GROUPS - 1):
        peer = (here + k + 1) % GROUPS
        along_pts(picked.at[peer], rows_in.at[k], c_send.at[0], c_recv.at[0], peer).start()

    def norms_of(low, high):
        def scoped(accs):
            quarter = jnp.full((32, TILE), -0.25, BF16)

            def some(i, carry):
                for h in range(0, PIECES, 4):
                    for q in range(h, h + 4):
                        rows = halves(xm[pl.ds(i * STEP + q * TILE, TILE), :])
                        pltpu.matmul_push_rhs(rows, q // 2 % 2, q % 2, transpose=True)
                        pltpu.matmul_acc_lhs(accs[q % 4], quarter, q // 2 % 2)
                    for q in range(h, h + 4):
                        sq[i, :, pl.ds(q * TILE, TILE)] = pltpu.matmul_pop(accs[q % 4])[:1]
                return carry

            lax.fori_loop(low, high, some, 0)

        pl.run_scoped(scoped, [pltpu.ACC(q % 2)((32, TILE), F32) for q in range(4)])

    norms_of(0, steps // 2)
    along_pts(rows_in, rows_in, c_send.at[0], c_recv.at[0], here).wait_recv()
    total = picked[here].astype(F32)
    for k in range(GROUPS - 1):
        total = total + rows_in[k].astype(F32)
    centers[here] = total.astype(BF16)
    for k in range(GROUPS - 1):
        peer = (here + k + 1) % GROUPS
        along_pts(centers.at[here], centers.at[here], c_send.at[1], c_recv.at[1], peer).start()
    norms_of(steps // 2, steps)
    ct[...] = coef[...].astype(F32).T.astype(BF16)
    pb1[...] = jnp.zeros_like(pb1)
    along_pts(rows_in, rows_in, c_send.at[1], c_recv.at[1], here).wait_recv()
    for g in range(GROUPS):
        rows_f = centers[g].astype(F32)
        ca[pl.ds(g * 128, 128), pl.ds(0, 128)] = (0.5 * rows_f).astype(BF16)
        ca[pl.ds(g * 128, 128), pl.ds(128, 128)] = augment(rows_f)

    def copy1(b):
        mine = part.at[pl.ds(2 + b * PIECES + (1 - core) * GROUPS, GROUPS)]
        return along_lmk(mine, p1r.at[b], s1.at[b], r1.at[b], other)

    def copy4(b):
        half = fit.at[b, pl.ds(core * GROUPS, GROUPS)]
        return along_lmk(half, half, s4.at[b], r4.at[b], other)

    def all2(b):
        return along_lmk(p2r.at[b], p2r.at[b], s2.at[b], r2.at[b], other)

    def all3(b):
        return along_lmk(p2r.at[b], p2r.at[b], s3.at[b], r3.at[b], other)

    def send1(b):
        copy1(b).start()

    def send2(b):
        copy1(b).wait_recv()
        for g in range(GROUPS):
            own = part[2 + b * PIECES + core * GROUPS + g]
            p2s[b, g] = (own.astype(F32) + p1r[b, g].astype(F32)).astype(BF16)
        for k in range(GROUPS - 1):
            peer = (chip + k + 1) % GROUPS
            along_lmk(p2s.at[b, peer], p2r.at[b, k], s2.at[b], r2.at[b], peer * 2 + core).start()

    def send3(b):
        all2(b).wait_recv()
        total = p2s[b, chip].astype(F32)
        for k in range(GROUPS - 1):
            total = total + p2r[b, k].astype(F32)
        mine = core * GROUPS + chip
        fit[b, mine] = total.astype(BF16)
        for k in range(GROUPS - 1):
            peer = (chip + k + 1) % GROUPS
            along_lmk(fit.at[b, mine], fit.at[b, mine], s3.at[b], r3.at[b], peer * 2 + core).start()

    def send4(b):
        all3(b).wait_recv()
        copy4(b).start()

    lane = lax.broadcasted_iota(jnp.int32, (TILE, 128), 1)
    ones = jnp.where(lane < 3, 1.0, 0.0).astype(BF16)
    blank = jnp.zeros((TILE - outs, TILE), BF16)
    segs = marks // SEG

    def main(accs, kts):
        def push_points(unit, m, reg):
            at = pl.multiple_of((unit * 2 + m) * TILE, TILE)
            rows = jnp.concatenate([xm[pl.ds(at, TILE), :], ones], axis=1)
            pltpu.matmul_push_rhs(rows, reg, m, transpose=True)

        def push_tile(par, m, q, reg):
            pltpu.matmul_push_rhs(pb[par][m, pl.ds(q * TILE, TILE), :], reg, m)

        def push_fitted(b, i, c, m, reg):
            pltpu.matmul_push_rhs(jnp.concatenate([fit[b, i * 2 + c], blank], axis=0), reg, m, transpose=True)

        def first_product(unit, par, m, q, reg):
            acc = accs[m]["B"]
            pltpu.matmul_acc_lhs(acc, ct[:, pl.ds(q * TILE, TILE)], reg)
            if q == 3:
                part[unit * 2 + m] = pltpu.matmul_pop(acc).astype(BF16)

        def second_product(kt, i, c, m, reg):
            pltpu.matmul_acc_lhs(accs[m]["C"], kt[i, c, pl.ds(m * (marks // 2), marks // 2), :], reg)

        def unit_step(t, i, par, second):
            kt, old = kts[t % SLOTS], kts[(t - LAG) % SLOTS]
            unit = t * UNITS + i
            after = jnp.minimum(unit + 1, steps * UNITS - 1)
            norms = [sq[t, :, pl.ds(pl.multiple_of((i * 2 + m) * TILE, TILE), TILE)] for m in MXUS]

            def finish(m, s):
                tile = jnp.exp(pltpu.matmul_pop(accs[m]["A"][s % RING]) + norms[m]).astype(BF16)
                rows = pl.ds(s * SEG, SEG)
                kt[i, m, rows, :] = tile
                pb[par][m, rows, :] = tile

            def distances(m, low, high):
                for s in range(low, high):
                    if s >= RING:
                        finish(m, s - RING)
                    acc = accs[m]["A"][s % RING]
                    pltpu.matmul_acc_lhs(acc, ca[pl.ds(s * SEG, SEG), :], 0 if s == low else None)

            def tail():
                for s in range(segs - RING, segs):
                    for m in MXUS:
                        finish(m, s)

            def each(f, *args):
                for m in MXUS:
                    f(*(m if a is MXUS else a for a in args))

            each(distances, MXUS, 0, segs // 2 if second else segs)
            if second:
                b = t - LAG
                each(push_fitted, b, i, 0, MXUS, 0)
                each(first_product, unit, par, MXUS, 0, 1)
                each(push_tile, 1 - par, MXUS, 1, 1)
                each(second_product, old, i, 0, MXUS, 0)
                each(push_points, unit, MXUS, 0)
                each(first_product, unit, par, MXUS, 1, 1)
                each(push_tile, 1 - par, MXUS, 2, 1)
                each(distances, MXUS, segs // 2, segs)
                each(push_fitted, b, i, 1, MXUS, 0)
                each(first_product, unit, par, MXUS, 2, 1)
                each(push_tile, 1 - par, MXUS, 3, 1)
                each(second_product, old, i, 1, MXUS, 0)
                tail()
                each(push_points, after, MXUS, 0)
                each(first_product, unit, par, MXUS, 3, 1)
                each(push_tile, par, MXUS, 0, 1)
            else:
                each(push_tile, 1 - par, MXUS, 1, 0)
                each(first_product, unit, par, MXUS, 0, 1)
                each(push_tile, 1 - par, MXUS, 2, 1)
                each(first_product, unit, par, MXUS, 1, 0)
                each(push_tile, 1 - par, MXUS, 3, 0)
                each(first_product, unit, par, MXUS, 2, 1)
                tail()
                each(push_tile, par, MXUS, 0, 1)
                each(first_product, unit, par, MXUS, 3, 0)
                each(push_points, after, MXUS, 0)

        for m in MXUS:
            push_points(0, m, 0)
            push_tile(1, m, 0, 1)

        for t in range(steps):
            if t >= LAG:
                copy4(t - LAG).wait_recv()

            def pair(i, carry, t=t):
                if t >= 1:

                    @pl.when(i == 1)
                    def _():
                        send1(t - 1)
                        if t >= 2:
                            send3(t - 2)

                    @pl.when(i == 3)
                    def _():
                        send2(t - 1)
                        if t >= 2:
                            send4(t - 2)

                unit_step(t, i * 2, 0, t >= LAG)
                unit_step(t, i * 2 + 1, 1, t >= LAG)
                return carry

            lax.fori_loop(0, UNITS // 2, pair, 0)

        last = steps * UNITS
        for m in MXUS:
            pltpu.matmul_acc_lhs(accs[m]["A"][0], ca[pl.ds(0, SEG), :], 0)
            push_tile(1, m, 1, 0)
            first_product(last, 0, m, 0, 1)
            push_tile(1, m, 2, 1)
            first_product(last, 0, m, 1, 0)
            push_tile(1, m, 3, 0)
            first_product(last, 0, m, 2, 1)
            first_product(last, 0, m, 3, 0)
            pltpu.matmul_pop(accs[m]["A"][0])

        def second_only(b, low, high):
            kt = kts[b % SLOTS]
            for m in MXUS:
                push_fitted(b, low, 0, m, 0)
                push_fitted(b, low, 1, m, 1)

            def unit(i, carry):
                for c in range(2):
                    for m in MXUS:
                        second_product(kt, i, c, m, c)
                        push_fitted(b, i + 1, c, m, c)
                return carry

            lax.fori_loop(low, high - 1, unit, 0)
            for c in range(2):
                for m in MXUS:
                    second_product(kt, high - 1, c, m, c)

        b = steps - 1
        send1(b)
        send3(b - 1)
        copy4(b - 2).wait_recv()
        second_only(b - 2, 0, UNITS // 2)
        send2(b)
        send4(b - 1)
        second_only(b - 2, UNITS // 2, UNITS)
        send3(b)
        copy4(b - 1).wait_recv()
        second_only(b - 1, 0, UNITS // 2)
        send4(b)
        second_only(b - 1, UNITS // 2, UNITS)
        copy4(b).wait_recv()
        second_only(b, 0, UNITS)

        for m in MXUS:
            total = pltpu.matmul_pop(accs[m]["C"])
            for g in range(GROUPS // 2):
                prod_t[m * (GROUPS // 2) + g] = total[g * 128 : (g + 1) * 128, :128].T[:outs]

    def acc(m):
        of = pltpu.ACC(m)
        return {"A": [of((SEG, TILE), F32)] * RING, "B": of((outs, TILE), F32), "C": of((marks // 2, TILE), F32)}

    kt = pltpu.VMEM((UNITS, 2, marks, TILE), BF16)
    pl.run_scoped(main, [acc(m) for m in MXUS], [kt] * SLOTS)

    for k in range(GROUPS - 1):
        peer = (here + k + 1) % GROUPS
        along_pts(prod_t.at[peer], prod_in.at[k], o_send, o_recv, peer).start()

    def sent(b, carry):
        copy1(b).wait_send()
        all2(b).wait_send()
        all3(b).wait_send()
        copy4(b).wait_send()
        return carry

    lax.fori_loop(0, steps, sent, 0)
    for i in range(2):
        along_pts(rows_in, rows_in, c_send.at[i], c_recv.at[i], here).wait_send()
    along_pts(prod_in, prod_in, o_send, o_recv, here).wait_recv()
    total = prod_t[here]
    for k in range(GROUPS - 1):
        total = total + prod_in[k]
    out[...] = total.T * (1.0 / (steps * STEP * GROUPS))
    along_pts(prod_in, prod_in, o_send, o_recv, here).wait_send()


def per_device(points, landmark_ids, coefficients):
    pts_rows, width = points.shape
    marks, outs = coefficients.shape
    steps = pts_rows // STEP
    vmem = pl.BlockSpec(memory_space=pltpu.VMEM)
    dma = pltpu.SemaphoreType.DMA
    return pl.pallas_call(
        functools.partial(body, steps),
        out_shape=jax.ShapeDtypeStruct((marks // GROUPS, outs), F32),
        in_specs=[pl.BlockSpec(memory_space=pltpu.SMEM), vmem, pl.BlockSpec(memory_space=pl.ANY)],
        out_specs=vmem,
        scratch_shapes=[
            pltpu.VMEM((pts_rows, width), BF16),
            pltpu.VMEM((steps, 1, STEP), F32),
            pltpu.VMEM((marks, width + 128), BF16),
            pltpu.VMEM((outs, marks), BF16),
            pltpu.VMEM((marks, width), F32),
            pltpu.VMEM((GROUPS, marks // GROUPS, width), BF16),
            pltpu.VMEM((GROUPS - 1, marks // GROUPS, width), BF16),
            pltpu.VMEM((GROUPS, marks // GROUPS, width), BF16),
            pltpu.VMEM((2, marks, TILE), BF16),
            pltpu.VMEM((2, marks, TILE), BF16),
            pltpu.VMEM((2 + steps * PIECES, outs, TILE), BF16),
            pltpu.VMEM((steps, GROUPS, outs, TILE), BF16),
            pltpu.VMEM((steps, GROUPS, outs, TILE), BF16),
            pltpu.VMEM((steps, GROUPS - 1, outs, TILE), BF16),
            pltpu.VMEM((steps, PIECES, outs, TILE), BF16),
            pltpu.VMEM((GROUPS, outs, 128), F32),
            pltpu.VMEM((GROUPS - 1, outs, 128), F32),
            dma((steps,)),
            dma((2,)),
            dma((2,)),
        ]
        + [dma((steps,))] * 8
        + [dma(()), dma(())],
        compiler_params=pltpu.CompilerParams(collective_id=0, has_side_effects=True, vmem_limit_bytes=60 * 2**20),
    )(landmark_ids, coefficients, points)


def solution(mesh):
    placed = (P("pts", None), P("lmk"), P("lmk", None))
    with jax.sharding.use_abstract_mesh(mesh.abstract_mesh):
        return jax.shard_map(
            per_device, mesh=mesh, in_specs=placed, out_specs=P(("lmk", "pts"), None), check_vma=False
        )
```

time: 104 us -> 104 us (level)
  Pallas kernels: 92.3 us -> 101 us
  local copies, waits for them, and re-layouts: 8.85 us -> 3.19 us
  other arithmetic: 2.43 us -> 0 us
    pallas_call x1, Pallas kernels: 92.3 us -> 101 us  [per_device(): pl.pallas_call(functools.partial(body, steps), out_shape=jax.ShapeDtypeSt...]
    gather x1 -> x0, local copies, waits for them, and re-layouts: 7.33 us -> none  [per_device(): picked = jnp.take(points, jnp.clip(local_ids, 0, pts_rows - 1), axis=0)]
    unnamed x0 -> x1, local copies, waits for them, and re-layouts: none -> 1.67 us
where the time goes in v2:
time: 104 us
  Pallas kernels  101 us (97%)
  local copies, waits for them, and re-layouts  3.19 us (3%)
    pallas_call x1, Pallas kernels, per_device(): pl.pallas_call(functools.partial(body, steps), out_shape=jax.ShapeDtypeSt...  101 us

profile of v2, /device:TPU:1, one launch (start us, length us, event | category | flops | bytes accessed | tf_op | source)
XLA Modules:
  0.0 104.0 jit_solution(18203123605399275577)
XLA Ops:
  0.0 1.7 %copy.4.coef = bf16[1024,32]{1,0:T(8,128)(2,1)} copy(bf16[1024,32]{0,1:T(8,128)(2,1)} %param.5) | data formatting | bytes 131072 | tf_op args[2]
  1.7 100.8 %shard_map.37 = f32[128,32]{1,0:T(8,128)} custom-call(s32[1024]{0:T(1024)} %ids.1, bf16[1024,32]{1,0:T(8,128)(2,1)} %copy.4.coef, bf16[32768,128]{1,0:T(8,128)(2,1)} %points.1), custom_call_target="tpu_custom_call" | custom-call | tf_op jit(solution)/shard_map/pallas_call | solution.py:378
  102.5 1.5 %copy.5 = f32[128,32]{0,1:T(8,128)} copy(f32[128,32]{1,0:T(8,128)} %shard_map.37) | data formatting | bytes 32768 | tf_op jit(solution)/shard_map/pallas_call | solution.py:378

commit v3 on v2

--- a/solution.py
+++ b/solution.py
@@ -14,8 +14,9 @@
 UNITS = 8
 PIECES = 2 * UNITS
 STEP = PIECES * TILE
-SLOTS = 4
-LAG = 3
+HALF = UNITS // 2
+LAG = 8
+SLOTS = LAG + 1
 SEG, RING = 128, 3
 MXUS = (0, 1)
 
@@ -63,6 +64,12 @@
         pl.semaphore_signal(barrier, inc=1, device_id={"lmk": ((chip + k + 1) % GROUPS) * 2 + core}, device_id_type=MESH)
     pl.semaphore_signal(barrier, inc=1, device_id={"lmk": other}, device_id_type=MESH)
 
+    def along_pts(src, dst, send, recv, peer):
+        return pltpu.make_async_remote_copy(src, dst, send, recv, device_id={"pts": peer}, device_id_type=MESH)
+
+    def along_lmk(src, dst, send, recv, peer):
+        return pltpu.make_async_remote_copy(src, dst, send, recv, device_id={"lmk": peer}, device_id_type=MESH)
+
     def gather(xf):
         def widen(i, carry):
             load(i).wait()
@@ -73,30 +80,30 @@
 
         lax.fori_loop(0, steps, widen, 0)
 
-        def pick(i, carry):
-            first = pl.multiple_of(i * 32, 32)
-            for u in range(32):
-                at = ids[first + u] - here * slab
-                row = xf[pl.ds(jnp.clip(at, 0, slab - 1), 1), :]
-                picked_f[pl.ds(first + u, 1), :] = jnp.where((at >= 0) & (at < slab), row, 0.0)
+        def pick(k, carry):
+            peer = (here + k + 1) % GROUPS
+
+            def some(i, carry):
+                for u in range(32):
+                    row_at = i * 32 + u
+                    at = ids[peer * 128 + row_at] - here * slab
+                    row = xf[pl.ds(jnp.clip(at, 0, slab - 1), 1), :]
+                    picked_f[pl.ds(row_at, 1), :] = jnp.where((at >= 0) & (at < slab), row, 0.0)
+                return carry
+
+            lax.fori_loop(0, 4, some, 0)
+            picked[peer] = picked_f[...].astype(BF16)
+
+            @pl.when(k < GROUPS - 1)
+            def _():
+                along_pts(picked.at[peer], rows_in.at[k], c_send.at[0], c_recv.at[0], peer).start()
+
             return carry
 
-        lax.fori_loop(0, marks // 32, pick, 0)
+        pl.semaphore_wait(barrier, 2 * GROUPS - 1)
+        lax.fori_loop(0, GROUPS, pick, 0)
 
     pl.run_scoped(gather, pltpu.VMEM((slab, width), F32))
-    for g in range(GROUPS):
-        picked[g] = picked_f[pl.ds(g * 128, 128), :].astype(BF16)
-    pl.semaphore_wait(barrier, 2 * GROUPS - 1)
-
-    def along_pts(src, dst, send, recv, peer):
-        return pltpu.make_async_remote_copy(src, dst, send, recv, device_id={"pts": peer}, device_id_type=MESH)
-
-    def along_lmk(src, dst, send, recv, peer):
-        return pltpu.make_async_remote_copy(src, dst, send, recv, device_id={"lmk": peer}, device_id_type=MESH)
-
-    for k in range(GROUPS - 1):
-        peer = (here + k + 1) % GROUPS
-        along_pts(picked.at[peer], rows_in.at[k], c_send.at[0], c_recv.at[0], peer).start()
 
     def norms_of(low, high):
         def scoped(accs):
@@ -109,7 +116,7 @@
                         pltpu.matmul_push_rhs(rows, q // 2 % 2, q % 2, transpose=True)
                         pltpu.matmul_acc_lhs(accs[q % 4], quarter, q // 2 % 2)
                     for q in range(h, h + 4):
-                        sq[i, :, pl.ds(q * TILE, TILE)] = pltpu.matmul_pop(accs[q % 4])[:1]
+                        sq[i, pl.ds(q, 1), :] = pltpu.matmul_pop(accs[q % 4])[:1]
                 return carry
 
             lax.fori_loop(low, high, some, 0)
@@ -189,8 +196,9 @@
         def push_tile(par, m, q, reg):
             pltpu.matmul_push_rhs(pb[par][m, pl.ds(q * TILE, TILE), :], reg, m)
 
-        def push_fitted(b, i, c, m, reg):
-            pltpu.matmul_push_rhs(jnp.concatenate([fit[b, i * 2 + c], blank], axis=0), reg, m, transpose=True)
+        def push_fitted(unit, c, m, reg):
+            piece = fit[unit // UNITS, unit % UNITS * 2 + c]
+            pltpu.matmul_push_rhs(jnp.concatenate([piece, blank], axis=0), reg, m, transpose=True)
 
         def first_product(unit, par, m, q, reg):
             acc = accs[m]["B"]
@@ -201,11 +209,11 @@
         def second_product(kt, i, c, m, reg):
             pltpu.matmul_acc_lhs(accs[m]["C"], kt[i, c, pl.ds(m * (marks // 2), marks // 2), :], reg)
 
-        def unit_step(t, i, par, second):
-            kt, old = kts[t % SLOTS], kts[(t - LAG) % SLOTS]
-            unit = t * UNITS + i
+        def unit_step(h, i, par, second):
+            kt, old = kts[h % SLOTS], kts[(h - LAG) % SLOTS]
+            unit = h * HALF + i
             after = jnp.minimum(unit + 1, steps * UNITS - 1)
-            norms = [sq[t, :, pl.ds(pl.multiple_of((i * 2 + m) * TILE, TILE), TILE)] for m in MXUS]
+            norms = [sq[h // 2, pl.ds((unit % UNITS) * 2 + m, 1), :] for m in MXUS]
 
             def finish(m, s):
                 tile = jnp.exp(pltpu.matmul_pop(accs[m]["A"][s % RING]) + norms[m]).astype(BF16)
@@ -231,8 +239,8 @@
 
             each(distances, MXUS, 0, segs // 2 if second else segs)
             if second:
-                b = t - LAG
-                each(push_fitted, b, i, 0, MXUS, 0)
+                before = unit - LAG * HALF
+                each(push_fitted, before, 0, MXUS, 0)
                 each(first_product, unit, par, MXUS, 0, 1)
                 each(push_tile, 1 - par, MXUS, 1, 1)
                 each(second_product, old, i, 0, MXUS, 0)
@@ -240,7 +248,7 @@
                 each(first_product, unit, par, MXUS, 1, 1)
                 each(push_tile, 1 - par, MXUS, 2, 1)
                 each(distances, MXUS, segs // 2, segs)
-                each(push_fitted, b, i, 1, MXUS, 0)
+                each(push_fitted, before, 1, MXUS, 0)
                 each(first_product, unit, par, MXUS, 2, 1)
                 each(push_tile, 1 - par, MXUS, 3, 1)
                 each(second_product, old, i, 1, MXUS, 0)
@@ -264,30 +272,24 @@
             push_points(0, m, 0)
             push_tile(1, m, 0, 1)
 
-        for t in range(steps):
-            if t >= LAG:
-                copy4(t - LAG).wait_recv()
-
-            def pair(i, carry, t=t):
-                if t >= 1:
-
-                    @pl.when(i == 1)
-                    def _():
-                        send1(t - 1)
-                        if t >= 2:
-                            send3(t - 2)
-
-                    @pl.when(i == 3)
-                    def _():
-                        send2(t - 1)
-                        if t >= 2:
-                            send4(t - 2)
-
-                unit_step(t, i * 2, 0, t >= LAG)
-                unit_step(t, i * 2 + 1, 1, t >= LAG)
+        def exchange(h):
+            for stage, behind in ((send2, 3), (send3, 5), (send4, 7)):
+                if h % 2 and 0 <= h - behind < 2 * steps:
+                    stage((h - behind) // 2)
+            if h % 2 == 0 and h >= LAG:
+                copy4((h - LAG) // 2).wait_recv()
+
+        for h in range(2 * steps):
+            exchange(h)
+
+            def pair(i, carry, h=h):
+                if h % 2 == 0 and h >= 2:
+                    pl.when(i == 1)(functools.partial(send1, h // 2 - 1))
+                unit_step(h, i * 2, 0, h >= LAG)
+                unit_step(h, i * 2 + 1, 1, h >= LAG)
                 return carry
 
-            lax.fori_loop(0, UNITS // 2, pair, 0)
+            lax.fori_loop(0, HALF // 2, pair, 0)
 
         last = steps * UNITS
         for m in MXUS:
@@ -301,39 +303,28 @@
             first_product(last, 0, m, 3, 0)
             pltpu.matmul_pop(accs[m]["A"][0])
 
-        def second_only(b, low, high):
-            kt = kts[b % SLOTS]
-            for m in MXUS:
-                push_fitted(b, low, 0, m, 0)
-                push_fitted(b, low, 1, m, 1)
+        def second_only(h):
+            kt, first = kts[h % SLOTS], h * HALF
+            for c in range(2):
+                for m in MXUS:
+                    push_fitted(first, c, m, c)
 
             def unit(i, carry):
                 for c in range(2):
                     for m in MXUS:
                         second_product(kt, i, c, m, c)
-                        push_fitted(b, i + 1, c, m, c)
+                        push_fitted(first + i + 1, c, m, c)
                 return carry
 
-            lax.fori_loop(low, high - 1, unit, 0)
+            lax.fori_loop(0, HALF - 1, unit, 0)
             for c in range(2):
                 for m in MXUS:
-                    second_product(kt, high - 1, c, m, c)
-
-        b = steps - 1
-        send1(b)
-        send3(b - 1)
-        copy4(b - 2).wait_recv()
-        second_only(b - 2, 0, UNITS // 2)
-        send2(b)
-        send4(b - 1)
-        second_only(b - 2, UNITS // 2, UNITS)
-        send3(b)
-        copy4(b - 1).wait_recv()
-        second_only(b - 1, 0, UNITS // 2)
-        send4(b)
-        second_only(b - 1, UNITS // 2, UNITS)
-        copy4(b).wait_recv()
-        second_only(b, 0, UNITS)
+                    second_product(kt, HALF - 1, c, m, c)
+
+        send1(steps - 1)
+        for h in range(2 * steps, 2 * steps + LAG):
+            exchange(h)
+            second_only(h - LAG)
 
         for m in MXUS:
             total = pltpu.matmul_pop(accs[m]["C"])
@@ -344,7 +335,7 @@
         of = pltpu.ACC(m)
         return {"A": [of((SEG, TILE), F32)] * RING, "B": of((outs, TILE), F32), "C": of((marks // 2, TILE), F32)}
 
-    kt = pltpu.VMEM((UNITS, 2, marks, TILE), BF16)
+    kt = pltpu.VMEM((HALF, 2, marks, TILE), BF16)
     pl.run_scoped(main, [acc(m) for m in MXUS], [kt] * SLOTS)
 
     for k in range(GROUPS - 1):
@@ -382,10 +373,10 @@
         out_specs=vmem,
         scratch_shapes=[
             pltpu.VMEM((pts_rows, width), BF16),
-            pltpu.VMEM((steps, 1, STEP), F32),
+            pltpu.VMEM((steps, PIECES, TILE), F32),
             pltpu.VMEM((marks, width + 128), BF16),
             pltpu.VMEM((outs, marks), BF16),
-            pltpu.VMEM((marks, width), F32),
+            pltpu.VMEM((marks // GROUPS, width), F32),
             pltpu.VMEM((GROUPS, marks // GROUPS, width), BF16),
             pltpu.VMEM((GROUPS - 1, marks // GROUPS, width), BF16),
             pltpu.VMEM((GROUPS, marks // GROUPS, width), BF16),

time: 104 us -> 89.9 us (0.86)
  Pallas kernels: 101 us -> 86.5 us
    pallas_call x1, Pallas kernels: 101 us -> 86.5 us  [per_device(): pl.pallas_call(functools.partial(body, steps), out_shape=jax.ShapeDtypeSt...]
where the time goes in v3:
time: 89.9 us; the launch traced here: 89.7 us
  Pallas kernels  86.5 us (96%)
  local copies, waits for them, and re-layouts  3.19 us (4%)
    pallas_call x1, Pallas kernels, per_device(): pl.pallas_call(functools.partial(body, steps), out_shape=jax.ShapeDtypeSt...  86.5 us

profile of v3, /device:TPU:1, one launch (start us, length us, event | category | flops | bytes accessed | tf_op | source)
XLA Modules:
  0.0 89.7 jit_solution(14037276643447741912)
XLA Ops:
  0.0 1.7 %copy.4.coef = bf16[1024,32]{1,0:T(8,128)(2,1)} copy(bf16[1024,32]{0,1:T(8,128)(2,1)} %param.5) | data formatting | bytes 131072 | tf_op args[2]
  1.7 86.5 %shard_map.37 = f32[128,32]{1,0:T(8,128)} custom-call(s32[1024]{0:T(1024)} %ids.1, bf16[1024,32]{1,0:T(8,128)(2,1)} %copy.4.coef, bf16[32768,128]{1,0:T(8,128)(2,1)} %points.1), custom_call_target="tpu_custom_call" | custom-call | tf_op jit(solution)/shard_map/pallas_call | solution.py:369
  88.1 1.5 %copy.5 = f32[128,32]{0,1:T(8,128)} copy(f32[128,32]{1,0:T(8,128)} %shard_map.37) | data formatting | bytes 32768 | tf_op jit(solution)/shard_map/pallas_call | solution.py:369

commit v4 on v3

--- a/solution.py
+++ b/solution.py
@@ -16,7 +16,8 @@
 STEP = PIECES * TILE
 HALF = UNITS // 2
 LAG = 8
-SLOTS = LAG + 1
+BACK = LAG * HALF + 1
+KEPT = (BACK + 1) // 2
 SEG, RING = 128, 3
 MXUS = (0, 1)
 
@@ -37,15 +38,14 @@
     return jnp.concatenate([hi, (squares - hi.astype(F32)).astype(BF16)], axis=1)
 
 
-def body(steps, ids, coef, points, out, xm, sq, ca, ct, picked_f, picked, rows_in, centers, pb0, pb1, part, p1r, p2s, p2r,
+def body(steps, ids, ct, points, out, xm, sq, ca, picked_f, picked, rows_in, centers, pb0, pb1, part, p1r, p2s, p2r,
          fit, prod_t, prod_in, load_sem, c_send, c_recv, s1, r1, s2, r2, s3, r3, s4, r4, o_send, o_recv):
     here = lax.axis_index("pts")
     lmk = lax.axis_index("lmk")
     chip, core = lmk // 2, lmk % 2
     other = chip * 2 + 1 - core
     slab, width = xm.shape
-    marks = coef.shape[0]
-    outs = coef.shape[1]
+    outs, marks = ct.shape
     pb = (pb0, pb1)
 
     def load(i):
@@ -133,7 +133,6 @@
         peer = (here + k + 1) % GROUPS
         along_pts(centers.at[here], centers.at[here], c_send.at[1], c_recv.at[1], peer).start()
     norms_of(steps // 2, steps)
-    ct[...] = coef[...].astype(F32).T.astype(BF16)
     pb1[...] = jnp.zeros_like(pb1)
     along_pts(rows_in, rows_in, c_send.at[1], c_recv.at[1], here).wait_recv()
     for g in range(GROUPS):
@@ -146,7 +145,7 @@
         return along_lmk(mine, p1r.at[b], s1.at[b], r1.at[b], other)
 
     def copy4(b):
-        half = fit.at[b, pl.ds(core * GROUPS, GROUPS)]
+        half = fit.at[pl.ds(2 + b * PIECES + core * GROUPS, GROUPS)]
         return along_lmk(half, half, s4.at[b], r4.at[b], other)
 
     def all2(b):
@@ -172,11 +171,11 @@
         total = p2s[b, chip].astype(F32)
         for k in range(GROUPS - 1):
             total = total + p2r[b, k].astype(F32)
-        mine = core * GROUPS + chip
-        fit[b, mine] = total.astype(BF16)
+        mine = 2 + b * PIECES + core * GROUPS + chip
+        fit[mine] = total.astype(BF16)
         for k in range(GROUPS - 1):
             peer = (chip + k + 1) % GROUPS
-            along_lmk(fit.at[b, mine], fit.at[b, mine], s3.at[b], r3.at[b], peer * 2 + core).start()
+            along_lmk(fit.at[mine], fit.at[mine], s3.at[b], r3.at[b], peer * 2 + core).start()
 
     def send4(b):
         all3(b).wait_recv()
@@ -197,8 +196,7 @@
             pltpu.matmul_push_rhs(pb[par][m, pl.ds(q * TILE, TILE), :], reg, m)
 
         def push_fitted(unit, c, m, reg):
-            piece = fit[unit // UNITS, unit % UNITS * 2 + c]
-            pltpu.matmul_push_rhs(jnp.concatenate([piece, blank], axis=0), reg, m, transpose=True)
+            pltpu.matmul_push_rhs(jnp.concatenate([fit[2 + unit * 2 + c], blank], axis=0), reg, m, transpose=True)
 
         def first_product(unit, par, m, q, reg):
             acc = accs[m]["B"]
@@ -206,19 +204,20 @@
             if q == 3:
                 part[unit * 2 + m] = pltpu.matmul_pop(acc).astype(BF16)
 
-        def second_product(kt, i, c, m, reg):
-            pltpu.matmul_acc_lhs(accs[m]["C"], kt[i, c, pl.ds(m * (marks // 2), marks // 2), :], reg)
+        def second_product(unit, par, c, m, reg):
+            tile = kts[par][lax.rem(unit // 2 + KEPT, KEPT), c, pl.ds(m * (marks // 2), marks // 2), :]
+            pltpu.matmul_acc_lhs(accs[m]["C"], tile, reg)
 
         def unit_step(h, i, par, second):
-            kt, old = kts[h % SLOTS], kts[(h - LAG) % SLOTS]
             unit = h * HALF + i
+            slot = lax.rem(unit // 2, KEPT)
             after = jnp.minimum(unit + 1, steps * UNITS - 1)
-            norms = [sq[h // 2, pl.ds((unit % UNITS) * 2 + m, 1), :] for m in MXUS]
+            norms = [sq[unit // UNITS, pl.ds((unit % UNITS) * 2 + m, 1), :] for m in MXUS]
 
             def finish(m, s):
                 tile = jnp.exp(pltpu.matmul_pop(accs[m]["A"][s % RING]) + norms[m]).astype(BF16)
                 rows = pl.ds(s * SEG, SEG)
-                kt[i, m, rows, :] = tile
+                kts[par][slot, m, rows, :] = tile
                 pb[par][m, rows, :] = tile
 
             def distances(m, low, high):
@@ -239,11 +238,11 @@
 
             each(distances, MXUS, 0, segs // 2 if second else segs)
             if second:
-                before = unit - LAG * HALF
+                before = unit - BACK
                 each(push_fitted, before, 0, MXUS, 0)
                 each(first_product, unit, par, MXUS, 0, 1)
                 each(push_tile, 1 - par, MXUS, 1, 1)
-                each(second_product, old, i, 0, MXUS, 0)
+                each(second_product, before, 1 - par, 0, MXUS, 0)
                 each(push_points, unit, MXUS, 0)
                 each(first_product, unit, par, MXUS, 1, 1)
                 each(push_tile, 1 - par, MXUS, 2, 1)
@@ -251,7 +250,7 @@
                 each(push_fitted, before, 1, MXUS, 0)
                 each(first_product, unit, par, MXUS, 2, 1)
                 each(push_tile, 1 - par, MXUS, 3, 1)
-                each(second_product, old, i, 1, MXUS, 0)
+                each(second_product, before, 1 - par, 1, MXUS, 0)
                 tail()
                 each(push_points, after, MXUS, 0)
                 each(first_product, unit, par, MXUS, 3, 1)
@@ -274,22 +273,40 @@
 
         def exchange(h):
             for stage, behind in ((send2, 3), (send3, 5), (send4, 7)):
-                if h % 2 and 0 <= h - behind < 2 * steps:
-                    stage((h - behind) // 2)
-            if h % 2 == 0 and h >= LAG:
-                copy4((h - LAG) // 2).wait_recv()
-
-        for h in range(2 * steps):
-            exchange(h)
-
-            def pair(i, carry, h=h):
-                if h % 2 == 0 and h >= 2:
-                    pl.when(i == 1)(functools.partial(send1, h // 2 - 1))
-                unit_step(h, i * 2, 0, h >= LAG)
-                unit_step(h, i * 2 + 1, 1, h >= LAG)
-                return carry
-
-            lax.fori_loop(0, HALF // 2, pair, 0)
+                due = (h % 2 == 1) & (h >= behind) & (h < behind + 2 * steps)
+                pl.when(due)(functools.partial(stage, (h - behind) // 2))
+
+        def tiles(low, high, second):
+            def half(h, carry):
+                exchange(h)
+                if second:
+                    pl.when(h % 2 == 0)(lambda: copy4((h - LAG) // 2).wait_recv())
+
+                def pair(i, carry):
+                    pl.when((i == 1) & (h % 2 == 0) & (h >= 2))(functools.partial(send1, h // 2 - 1))
+                    unit_step(h, i * 2, 0, second)
+                    unit_step(h, i * 2 + 1, 1, second)
+                    return carry
+
+                return lax.fori_loop(0, HALF // 2, pair, carry)
+
+            lax.fori_loop(low, high, half, 0)
+
+        kts[1][KEPT - 1] = jnp.zeros((2, marks, TILE), BF16)
+        fit[pl.ds(0, 2)] = jnp.zeros((2, outs, TILE), BF16)
+        tiles(0, LAG, False)
+        tiles(LAG, 2 * steps, True)
+
+        def second_only(first, count):
+            turns = [(first + i, (count + i) % 2, c) for i in range(count) for c in range(2)]
+            for unit, _, c in turns[:2]:
+                for m in MXUS:
+                    push_fitted(unit, c, m, c)
+            for at, (unit, par, c) in enumerate(turns):
+                for m in MXUS:
+                    second_product(unit, par, c, m, c)
+                    if at + 2 < len(turns):
+                        push_fitted(turns[at + 2][0], c, m, c)
 
         last = steps * UNITS
         for m in MXUS:
@@ -303,28 +320,15 @@
             first_product(last, 0, m, 3, 0)
             pltpu.matmul_pop(accs[m]["A"][0])
 
-        def second_only(h):
-            kt, first = kts[h % SLOTS], h * HALF
-            for c in range(2):
-                for m in MXUS:
-                    push_fitted(first, c, m, c)
-
-            def unit(i, carry):
-                for c in range(2):
-                    for m in MXUS:
-                        second_product(kt, i, c, m, c)
-                        push_fitted(first + i + 1, c, m, c)
-                return carry
-
-            lax.fori_loop(0, HALF - 1, unit, 0)
-            for c in range(2):
-                for m in MXUS:
-                    second_product(kt, HALF - 1, c, m, c)
+        def rest(h, carry):
+            exchange(h)
+            pl.when(h % 2 == 0)(lambda: copy4((h - LAG) // 2).wait_recv())
+            second_only((h - LAG) * HALF, HALF)
+            return carry
 
         send1(steps - 1)
-        for h in range(2 * steps, 2 * steps + LAG):
-            exchange(h)
-            second_only(h - LAG)
+        second_only((2 * steps - LAG) * HALF - 1, 1)
+        lax.fori_loop(2 * steps, 2 * steps + LAG, rest, 0)
 
         for m in MXUS:
             total = pltpu.matmul_pop(accs[m]["C"])
@@ -335,8 +339,7 @@
         of = pltpu.ACC(m)
         return {"A": [of((SEG, TILE), F32)] * RING, "B": of((outs, TILE), F32), "C": of((marks // 2, TILE), F32)}
 
-    kt = pltpu.VMEM((HALF, 2, marks, TILE), BF16)
-    pl.run_scoped(main, [acc(m) for m in MXUS], [kt] * SLOTS)
+    pl.run_scoped(main, [acc(m) for m in MXUS], [pltpu.VMEM((KEPT, 2, marks, TILE), BF16)] * 2)
 
     for k in range(GROUPS - 1):
         peer = (here + k + 1) % GROUPS
@@ -356,7 +359,7 @@
     total = prod_t[here]
     for k in range(GROUPS - 1):
         total = total + prod_in[k]
-    out[...] = total.T * (1.0 / (steps * STEP * GROUPS))
+    out[...] = total
     along_pts(prod_in, prod_in, o_send, o_recv, here).wait_send()
 
 
@@ -366,16 +369,15 @@
     steps = pts_rows // STEP
     vmem = pl.BlockSpec(memory_space=pltpu.VMEM)
     dma = pltpu.SemaphoreType.DMA
-    return pl.pallas_call(
+    product = pl.pallas_call(
         functools.partial(body, steps),
-        out_shape=jax.ShapeDtypeStruct((marks // GROUPS, outs), F32),
+        out_shape=jax.ShapeDtypeStruct((outs, marks // GROUPS), F32),
         in_specs=[pl.BlockSpec(memory_space=pltpu.SMEM), vmem, pl.BlockSpec(memory_space=pl.ANY)],
         out_specs=vmem,
         scratch_shapes=[
             pltpu.VMEM((pts_rows, width), BF16),
             pltpu.VMEM((steps, PIECES, TILE), F32),
             pltpu.VMEM((marks, width + 128), BF16),
-            pltpu.VMEM((outs, marks), BF16),
             pltpu.VMEM((marks // GROUPS, width), F32),
             pltpu.VMEM((GROUPS, marks // GROUPS, width), BF16),
             pltpu.VMEM((GROUPS - 1, marks // GROUPS, width), BF16),
@@ -386,7 +388,7 @@
             pltpu.VMEM((steps, GROUPS, outs, TILE), BF16),
             pltpu.VMEM((steps, GROUPS, outs, TILE), BF16),
             pltpu.VMEM((steps, GROUPS - 1, outs, TILE), BF16),
-            pltpu.VMEM((steps, PIECES, outs, TILE), BF16),
+            pltpu.VMEM((2 + steps * PIECES, outs, TILE), BF16),
             pltpu.VMEM((GROUPS, outs, 128), F32),
             pltpu.VMEM((GROUPS - 1, outs, 128), F32),
             dma((steps,)),
@@ -396,7 +398,8 @@
         + [dma((steps,))] * 8
         + [dma(()), dma(())],
         compiler_params=pltpu.CompilerParams(collective_id=0, has_side_effects=True, vmem_limit_bytes=60 * 2**20),
-    )(landmark_ids, coefficients, points)
+    )(landmark_ids, coefficients.T, points)
+    return product.T / (pts_rows * GROUPS)
 
 
 def solution(mesh):

time: 89.9 us -> 88.7 us (0.987)
  local copies, waits for them, and re-layouts: 3.19 us -> 0 us
  other arithmetic: 0 us -> 1.33 us
    unnamed x1 -> x0, local copies, waits for them, and re-layouts: 1.67 us -> none
    pallas_call x1 -> x0, local copies, waits for them, and re-layouts: 1.52 us -> none  [per_device(): pl.pallas_call(functools.partial(body, steps), out_shape=jax.ShapeDtypeSt...]
    div x0 -> x1, other arithmetic: none -> 1.33 us  [per_device(): return product.T / (pts_rows * GROUPS)]
where the time goes in v4:
time: 88.7 us; the launch traced here: 88.5 us
  Pallas kernels  87.2 us (98%)
  other arithmetic  1.33 us (1%)
    pallas_call x1, Pallas kernels, per_device(): pl.pallas_call(functools.partial(body, steps), out_shape=jax.ShapeDtypeSt...  87.2 us

profile of v4, /device:TPU:1, one launch (start us, length us, event | category | flops | bytes accessed | tf_op | source)
XLA Modules:
  0.0 88.5 jit_solution(7918976864377415879)
XLA Ops:
  0.0 87.2 %shard_map.37 = f32[32,128]{1,0:T(8,128)} custom-call(s32[1024]{0:T(1024)} %ids.1, bf16[32,1024]{1,0:T(8,128)(2,1)} %bitcast.3, bf16[32768,128]{1,0:T(8,128)(2,1)} %points.1), custom_call_target="tpu_custom_call" | custom-call | tf_op jit(solution)/shard_map/pallas_call | solution.py:372
  87.2 1.3 %multiply_bitcast_fusion = f32[128,32]{0,1:T(8,128)} fusion(f32[32,128]{1,0:T(8,128)} %shard_map.37), kind=kLoop, calls=%fused_computation | loop fusion | flops 4096 | bytes 32768 | tf_op jit(solution)/shard_map/div | solution.py:402

commit v5 on v4

--- a/solution.py
+++ b/solution.py
@@ -16,8 +16,9 @@
 STEP = PIECES * TILE
 HALF = UNITS // 2
 LAG = 8
-BACK = LAG * HALF + 1
+BACK = LAG * HALF + 3
 KEPT = (BACK + 1) // 2
+BLANK = 2 * (BACK - LAG * HALF)
 SEG, RING = 128, 3
 MXUS = (0, 1)
 
@@ -145,7 +146,7 @@
         return along_lmk(mine, p1r.at[b], s1.at[b], r1.at[b], other)
 
     def copy4(b):
-        half = fit.at[pl.ds(2 + b * PIECES + core * GROUPS, GROUPS)]
+        half = fit.at[pl.ds(BLANK + b * PIECES + core * GROUPS, GROUPS)]
         return along_lmk(half, half, s4.at[b], r4.at[b], other)
 
     def all2(b):
@@ -171,7 +172,7 @@
         total = p2s[b, chip].astype(F32)
         for k in range(GROUPS - 1):
             total = total + p2r[b, k].astype(F32)
-        mine = 2 + b * PIECES + core * GROUPS + chip
+        mine = BLANK + b * PIECES + core * GROUPS + chip
         fit[mine] = total.astype(BF16)
         for k in range(GROUPS - 1):
             peer = (chip + k + 1) % GROUPS
@@ -196,7 +197,7 @@
             pltpu.matmul_push_rhs(pb[par][m, pl.ds(q * TILE, TILE), :], reg, m)
 
         def push_fitted(unit, c, m, reg):
-            pltpu.matmul_push_rhs(jnp.concatenate([fit[2 + unit * 2 + c], blank], axis=0), reg, m, transpose=True)
+            pltpu.matmul_push_rhs(jnp.concatenate([fit[BLANK + unit * 2 + c], blank], axis=0), reg, m, transpose=True)
 
         def first_product(unit, par, m, q, reg):
             acc = accs[m]["B"]
@@ -236,7 +237,7 @@
                 for m in MXUS:
                     f(*(m if a is MXUS else a for a in args))
 
-            each(distances, MXUS, 0, segs // 2 if second else segs)
+            each(distances, MXUS, 0, segs // 2 if second else 3)
             if second:
                 before = unit - BACK
                 each(push_fitted, before, 0, MXUS, 0)
@@ -256,10 +257,14 @@
                 each(first_product, unit, par, MXUS, 3, 1)
                 each(push_tile, par, MXUS, 0, 1)
             else:
-                each(push_tile, 1 - par, MXUS, 1, 0)
+                each(push_points, unit, MXUS, 0)
                 each(first_product, unit, par, MXUS, 0, 1)
+                each(push_tile, 1 - par, MXUS, 1, 1)
+                each(distances, MXUS, 3, 6)
+                each(push_points, unit, MXUS, 0)
+                each(first_product, unit, par, MXUS, 1, 1)
                 each(push_tile, 1 - par, MXUS, 2, 1)
-                each(first_product, unit, par, MXUS, 1, 0)
+                each(distances, MXUS, 6, segs)
                 each(push_tile, 1 - par, MXUS, 3, 0)
                 each(first_product, unit, par, MXUS, 2, 1)
                 tail()
@@ -278,12 +283,14 @@
 
         def tiles(low, high, second):
             def half(h, carry):
-                exchange(h)
-                if second:
-                    pl.when(h % 2 == 0)(lambda: copy4((h - LAG) // 2).wait_recv())
-
                 def pair(i, carry):
-                    pl.when((i == 1) & (h % 2 == 0) & (h >= 2))(functools.partial(send1, h // 2 - 1))
+                    @pl.when(i == 1)
+                    def _():
+                        pl.when((h % 2 == 0) & (h >= 2))(functools.partial(send1, h // 2 - 1))
+                        exchange(h)
+                        if second:
+                            pl.when(h % 2 == 0)(lambda: copy4((h - LAG) // 2).wait_recv())
+
                     unit_step(h, i * 2, 0, second)
                     unit_step(h, i * 2 + 1, 1, second)
                     return carry
@@ -292,8 +299,9 @@
 
             lax.fori_loop(low, high, half, 0)
 
-        kts[1][KEPT - 1] = jnp.zeros((2, marks, TILE), BF16)
-        fit[pl.ds(0, 2)] = jnp.zeros((2, outs, TILE), BF16)
+        for unit in range(LAG * HALF - BACK, 0):
+            kts[unit % 2][unit // 2 + KEPT] = jnp.zeros((2, marks, TILE), BF16)
+        fit[pl.ds(0, BLANK)] = jnp.zeros((BLANK, outs, TILE), BF16)
         tiles(0, LAG, False)
         tiles(LAG, 2 * steps, True)
 
@@ -327,7 +335,8 @@
             return carry
 
         send1(steps - 1)
-        second_only((2 * steps - LAG) * HALF - 1, 1)
+        ahead = BACK - LAG * HALF
+        second_only((2 * steps - LAG) * HALF - ahead, ahead)
         lax.fori_loop(2 * steps, 2 * steps + LAG, rest, 0)
 
         for m in MXUS:
@@ -388,7 +397,7 @@
             pltpu.VMEM((steps, GROUPS, outs, TILE), BF16),
             pltpu.VMEM((steps, GROUPS, outs, TILE), BF16),
             pltpu.VMEM((steps, GROUPS - 1, outs, TILE), BF16),
-            pltpu.VMEM((2 + steps * PIECES, outs, TILE), BF16),
+            pltpu.VMEM((BLANK + steps * PIECES, outs, TILE), BF16),
             pltpu.VMEM((GROUPS, outs, 128), F32),
             pltpu.VMEM((GROUPS - 1, outs, 128), F32),
             dma((steps,)),

time: 88.7 us -> 85.5 us (0.964)
  Pallas kernels: 87.2 us -> 84 us
    pallas_call x1, Pallas kernels: 87.2 us -> 84 us  [per_device(): pl.pallas_call(functools.partial(body, steps), out_shape=jax.ShapeDtypeSt...]
where the time goes in v5:
time: 85.5 us; the launch traced here: 85.3 us
  Pallas kernels  84 us (98%)
  other arithmetic  1.33 us (2%)
    pallas_call x1, Pallas kernels, per_device(): pl.pallas_call(functools.partial(body, steps), out_shape=jax.ShapeDtypeSt...  84 us

profile of v5, /device:TPU:1, one launch (start us, length us, event | category | flops | bytes accessed | tf_op | source)
XLA Modules:
  0.0 85.3 jit_solution(7933334183984748422)
XLA Ops:
  0.0 84.0 %shard_map.37 = f32[32,128]{1,0:T(8,128)} custom-call(s32[1024]{0:T(1024)} %ids.1, bf16[32,1024]{1,0:T(8,128)(2,1)} %bitcast.3, bf16[32768,128]{1,0:T(8,128)(2,1)} %points.1), custom_call_target="tpu_custom_call" | custom-call | tf_op jit(solution)/shard_map/pallas_call | solution.py:381
  84.0 1.3 %multiply_bitcast_fusion = f32[128,32]{0,1:T(8,128)} fusion(f32[32,128]{1,0:T(8,128)} %shard_map.37), kind=kLoop, calls=%fused_computation | loop fusion | flops 4096 | bytes 32768 | tf_op jit(solution)/shard_map/div | solution.py:411

commit v6 on v5

--- a/solution.py
+++ b/solution.py
@@ -19,7 +19,7 @@
 BACK = LAG * HALF + 3
 KEPT = (BACK + 1) // 2
 BLANK = 2 * (BACK - LAG * HALF)
-SEG, RING = 128, 3
+SEG, RING = 64, 7
 MXUS = (0, 1)
 
 
@@ -237,7 +237,7 @@
                 for m in MXUS:
                     f(*(m if a is MXUS else a for a in args))
 
-            each(distances, MXUS, 0, segs // 2 if second else 3)
+            each(distances, MXUS, 0, segs // 2 if second else 3 * segs // 8)
             if second:
                 before = unit - BACK
                 each(push_fitted, before, 0, MXUS, 0)
@@ -260,11 +260,11 @@
                 each(push_points, unit, MXUS, 0)
                 each(first_product, unit, par, MXUS, 0, 1)
                 each(push_tile, 1 - par, MXUS, 1, 1)
-                each(distances, MXUS, 3, 6)
+                each(distances, MXUS, 3 * segs // 8, 3 * segs // 4)
                 each(push_points, unit, MXUS, 0)
                 each(first_product, unit, par, MXUS, 1, 1)
                 each(push_tile, 1 - par, MXUS, 2, 1)
-                each(distances, MXUS, 6, segs)
+                each(distances, MXUS, 3 * segs // 4, segs)
                 each(push_tile, 1 - par, MXUS, 3, 0)
                 each(first_product, unit, par, MXUS, 2, 1)
                 tail()
@@ -329,7 +329,7 @@
             pltpu.matmul_pop(accs[m]["A"][0])
 
         def rest(h, carry):
-            exchange(h)
+            exchange(h + 1)
             pl.when(h % 2 == 0)(lambda: copy4((h - LAG) // 2).wait_recv())
             second_only((h - LAG) * HALF, HALF)
             return carry

time: 85.5 us -> 83.6 us (0.978); the launches traced: 85.3 us -> 82.4 us
  Pallas kernels: 84 us -> 81.1 us
    pallas_call x1, Pallas kernels: 84 us -> 81.1 us  [per_device(): pl.pallas_call(functools.partial(body, steps), out_shape=jax.ShapeDtypeSt...]
where the time goes in v6:
time: 83.6 us; the launch traced here: 82.4 us
  Pallas kernels  81.1 us (97%)
  other arithmetic  1.33 us (2%)
    pallas_call x1, Pallas kernels, per_device(): pl.pallas_call(functools.partial(body, steps), out_shape=jax.ShapeDtypeSt...  81.1 us

profile of v6, /device:TPU:1, one launch (start us, length us, event | category | flops | bytes accessed | tf_op | source)
XLA Modules:
  0.0 82.4 jit_solution(12122769509942804500)
XLA Ops:
  0.0 81.1 %shard_map.37 = f32[32,128]{1,0:T(8,128)} custom-call(s32[1024]{0:T(1024)} %ids.1, bf16[32,1024]{1,0:T(8,128)(2,1)} %bitcast.3, bf16[32768,128]{1,0:T(8,128)(2,1)} %points.1), custom_call_target="tpu_custom_call" | custom-call | tf_op jit(solution)/shard_map/pallas_call | solution.py:381
  81.1 1.3 %multiply_bitcast_fusion = f32[128,32]{0,1:T(8,128)} fusion(f32[32,128]{1,0:T(8,128)} %shard_map.37), kind=kLoop, calls=%fused_computation | loop fusion | flops 4096 | bytes 32768 | tf_op jit(solution)/shard_map/div | solution.py:411

commit v7 on v6

--- a/solution.py
+++ b/solution.py
@@ -40,7 +40,7 @@
 
 
 def body(steps, ids, ct, points, out, xm, sq, ca, picked_f, picked, rows_in, centers, pb0, pb1, part, p1r, p2s, p2r,
-         fit, prod_t, prod_in, load_sem, c_send, c_recv, s1, r1, s2, r2, s3, r3, s4, r4, o_send, o_recv):
+         fit, end_in, prod_t, prod_in, load_sem, c_send, c_recv, s1, r1, s2, r2, s3, r3, s4, r4, e1, e2, e3, e4, o_send, o_recv):
     here = lax.axis_index("pts")
     lmk = lax.axis_index("lmk")
     chip, core = lmk // 2, lmk % 2
@@ -278,19 +278,63 @@
 
         def exchange(h):
             for stage, behind in ((send2, 3), (send3, 5), (send4, 7)):
-                due = (h % 2 == 1) & (h >= behind) & (h < behind + 2 * steps)
+                due = (h % 2 == 1) & (h >= behind)
                 pl.when(due)(functools.partial(stage, (h - behind) // 2))
+
+        end = steps - 1
+        lanes = pl.ds(pl.multiple_of(chip % 2 * 128, 128), 128)
+        share = GROUPS // 2
+
+        def end1(e):
+            mine = part.at[pl.ds(2 + end * PIECES + e * GROUPS + (1 - core) * share, share)]
+            return along_lmk(mine, p1r.at[end, pl.ds(e * share, share)], e1.at[0, e], e1.at[1, e], other)
+
+        def all_end(stage, e):
+            return along_lmk(end_in.at[e], end_in.at[e], stage.at[0, e], stage.at[1, e], other)
+
+        def end4(e):
+            half = fit.at[pl.ds(BLANK + end * PIECES + e * GROUPS + core * share, share)]
+            return along_lmk(half, half, e4.at[0, e], e4.at[1, e], other)
+
+        def end_send2(e):
+            end1(e).wait_recv()
+            for g in range(share):
+                own = part[2 + end * PIECES + e * GROUPS + core * share + g]
+                p2s[end, e * share + g] = (own.astype(F32) + p1r[end, e * share + g].astype(F32)).astype(BF16)
+            for k in range(GROUPS - 1):
+                peer = (chip + k + 1) % GROUPS
+                theirs = pl.ds(pl.multiple_of(peer % 2 * 128, 128), 128)
+                src = p2s.at[end, e * share + peer // 2, :, theirs]
+                along_lmk(src, end_in.at[e, k], e2.at[0, e], e2.at[1, e], peer * 2 + core).start()
+
+        def end_send3(e):
+            all_end(e2, e).wait_recv()
+            total = p2s[end, e * share + chip // 2, :, lanes].astype(F32)
+            for k in range(GROUPS - 1):
+                total = total + end_in[e, k].astype(F32)
+            mine = BLANK + end * PIECES + e * GROUPS + core * share + chip // 2
+            fit[mine, :, lanes] = total.astype(BF16)
+            for k in range(GROUPS - 1):
+                peer = (chip + k + 1) % GROUPS
+                piece = fit.at[mine, :, lanes]
+                along_lmk(piece, piece, e3.at[0, e], e3.at[1, e], peer * 2 + core).start()
+
+        def end_send4(e):
+            all_end(e3, e).wait_recv()
+            end4(e).start()
 
         def tiles(low, high, second):
             def half(h, carry):
                 def pair(i, carry):
-                    @pl.when(i == 1)
+                    @pl.when(((i == 1) & (h < 2 * steps - 1)) | ((i == 0) & (h == 2 * steps - 1)))
                     def _():
                         pl.when((h % 2 == 0) & (h >= 2))(functools.partial(send1, h // 2 - 1))
                         exchange(h)
                         if second:
                             pl.when(h % 2 == 0)(lambda: copy4((h - LAG) // 2).wait_recv())
 
+                    if second:
+                        pl.when((i == 1) & (h == 2 * steps - 1))(lambda: end1(0).start())
                     unit_step(h, i * 2, 0, second)
                     unit_step(h, i * 2 + 1, 1, second)
                     return carry
@@ -328,17 +372,37 @@
             first_product(last, 0, m, 3, 0)
             pltpu.matmul_pop(accs[m]["A"][0])
 
-        def rest(h, carry):
-            exchange(h + 1)
-            pl.when(h % 2 == 0)(lambda: copy4((h - LAG) // 2).wait_recv())
-            second_only((h - LAG) * HALF, HALF)
-            return carry
-
-        send1(steps - 1)
+        end1(1).start()
+        end_send2(0)
         ahead = BACK - LAG * HALF
         second_only((2 * steps - LAG) * HALF - ahead, ahead)
-        lax.fori_loop(2 * steps, 2 * steps + LAG, rest, 0)
-
+        end_send2(1)
+        copy4(end - 3).wait_recv()
+        second_only((2 * steps - LAG) * HALF, HALF)
+        send3(end - 1)
+        send4(end - 2)
+        second_only((2 * steps - LAG + 1) * HALF, HALF)
+        copy4(end - 2).wait_recv()
+        second_only((2 * steps - LAG + 2) * HALF, HALF)
+        end_send3(0)
+        end_send3(1)
+        second_only((2 * steps - LAG + 3) * HALF, HALF)
+        send4(end - 1)
+        copy4(end - 1).wait_recv()
+        second_only((2 * steps - LAG + 4) * HALF, HALF)
+        end_send4(0)
+        second_only((2 * steps - LAG + 5) * HALF, HALF)
+        end_send4(1)
+        end4(0).wait_recv()
+        second_only((2 * steps - LAG + 6) * HALF, HALF)
+        end4(1).wait_recv()
+        second_only((2 * steps - LAG + 7) * HALF, HALF)
+
+        for e in range(2):
+            end1(e).wait_send()
+            all_end(e2, e).wait_send()
+            all_end(e3, e).wait_send()
+            end4(e).wait_send()
         for m in MXUS:
             total = pltpu.matmul_pop(accs[m]["C"])
             for g in range(GROUPS // 2):
@@ -361,7 +425,7 @@
         copy4(b).wait_send()
         return carry
 
-    lax.fori_loop(0, steps, sent, 0)
+    lax.fori_loop(0, steps - 1, sent, 0)
     for i in range(2):
         along_pts(rows_in, rows_in, c_send.at[i], c_recv.at[i], here).wait_send()
     along_pts(prod_in, prod_in, o_send, o_recv, here).wait_recv()
@@ -398,6 +462,7 @@
             pltpu.VMEM((steps, GROUPS, outs, TILE), BF16),
             pltpu.VMEM((steps, GROUPS - 1, outs, TILE), BF16),
             pltpu.VMEM((BLANK + steps * PIECES, outs, TILE), BF16),
+            pltpu.VMEM((2, GROUPS - 1, outs, 128), BF16),
             pltpu.VMEM((GROUPS, outs, 128), F32),
             pltpu.VMEM((GROUPS - 1, outs, 128), F32),
             dma((steps,)),
@@ -405,6 +470,7 @@
             dma((2,)),
         ]
         + [dma((steps,))] * 8
+        + [dma((2, 2))] * 4
         + [dma(()), dma(())],
         compiler_params=pltpu.CompilerParams(collective_id=0, has_side_effects=True, vmem_limit_bytes=60 * 2**20),
     )(landmark_ids, coefficients.T, points)

time: 83.6 us -> 82.7 us (0.989); the launches traced: 82.4 us -> 82.5 us
  no operation moved by 1% of the time
where the time goes in v7:
time: 82.7 us; the launch traced here: 82.5 us
  Pallas kernels  81.2 us (98%)
  other arithmetic  1.33 us (2%)
    pallas_call x1, Pallas kernels, per_device(): pl.pallas_call(functools.partial(body, steps), out_shape=jax.ShapeDtypeSt...  81.2 us

profile of v7, /device:TPU:1, one launch (start us, length us, event | category | flops | bytes accessed | tf_op | source)
XLA Modules:
  0.0 82.5 jit_solution(6531473621237932634)
XLA Ops:
  0.0 81.2 %shard_map.37 = f32[32,128]{1,0:T(8,128)} custom-call(s32[1024]{0:T(1024)} %ids.1, bf16[32,1024]{1,0:T(8,128)(2,1)} %bitcast.3, bf16[32768,128]{1,0:T(8,128)(2,1)} %points.1), custom_call_target="tpu_custom_call" | custom-call | tf_op jit(solution)/shard_map/pallas_call | solution.py:445
  81.2 1.3 %multiply_bitcast_fusion = f32[128,32]{0,1:T(8,128)} fusion(f32[32,128]{1,0:T(8,128)} %shard_map.37), kind=kLoop, calls=%fused_computation | loop fusion | flops 4096 | bytes 32768 | tf_op jit(solution)/shard_map/div | solution.py:477

commit v8 on v7

--- a/solution.py
+++ b/solution.py
@@ -79,6 +79,7 @@
                 xf[rows, :] = xm[rows, :].astype(F32)
             return carry
 
+        xf[pl.ds(slab, 8), :] = jnp.zeros((8, width), F32)
         lax.fori_loop(0, steps, widen, 0)
 
         def pick(k, carry):
@@ -88,8 +89,8 @@
                 for u in range(32):
                     row_at = i * 32 + u
                     at = ids[peer * 128 + row_at] - here * slab
-                    row = xf[pl.ds(jnp.clip(at, 0, slab - 1), 1), :]
-                    picked_f[pl.ds(row_at, 1), :] = jnp.where((at >= 0) & (at < slab), row, 0.0)
+                    at = jnp.where((at >= 0) & (at < slab), at, slab)
+                    picked_f[pl.ds(row_at, 1), :] = xf[pl.ds(at, 1), :]
                 return carry
 
             lax.fori_loop(0, 4, some, 0)
@@ -104,7 +105,7 @@
         pl.semaphore_wait(barrier, 2 * GROUPS - 1)
         lax.fori_loop(0, GROUPS, pick, 0)
 
-    pl.run_scoped(gather, pltpu.VMEM((slab, width), F32))
+    pl.run_scoped(gather, pltpu.VMEM((slab + 8, width), F32))
 
     def norms_of(low, high):
         def scoped(accs):

time: 82.7 us -> 81.4 us (0.984)
  Pallas kernels: 81.2 us -> 79.9 us
    pallas_call x1, Pallas kernels: 81.2 us -> 79.9 us  [per_device(): pl.pallas_call(functools.partial(body, steps), out_shape=jax.ShapeDtypeSt...]
where the time goes in v8:
time: 81.4 us; the launch traced here: 81.2 us
  Pallas kernels  79.9 us (98%)
  other arithmetic  1.33 us (2%)
    pallas_call x1, Pallas kernels, per_device(): pl.pallas_call(functools.partial(body, steps), out_shape=jax.ShapeDtypeSt...  79.9 us

profile of v8, /device:TPU:1, one launch (start us, length us, event | category | flops | bytes accessed | tf_op | source)
XLA Modules:
  0.0 81.2 jit_solution(9620313548185807674)
XLA Ops:
  0.0 79.9 %shard_map.37 = f32[32,128]{1,0:T(8,128)} custom-call(s32[1024]{0:T(1024)} %ids.1, bf16[32,1024]{1,0:T(8,128)(2,1)} %bitcast.3, bf16[32768,128]{1,0:T(8,128)(2,1)} %points.1), custom_call_target="tpu_custom_call" | custom-call | tf_op jit(solution)/shard_map/pallas_call | solution.py:446
  79.9 1.3 %multiply_bitcast_fusion = f32[128,32]{0,1:T(8,128)} fusion(f32[32,128]{1,0:T(8,128)} %shard_map.37), kind=kLoop, calls=%fused_computation | loop fusion | flops 4096 | bytes 32768 | tf_op jit(solution)/shard_map/div | solution.py:478

commit v9 on v8

--- a/solution.py
+++ b/solution.py
@@ -125,7 +125,7 @@
 
         pl.run_scoped(scoped, [pltpu.ACC(q % 2)((32, TILE), F32) for q in range(4)])
 
-    norms_of(0, steps // 2)
+    norms_of(0, steps // 4)
     along_pts(rows_in, rows_in, c_send.at[0], c_recv.at[0], here).wait_recv()
     total = picked[here].astype(F32)
     for k in range(GROUPS - 1):
@@ -134,7 +134,7 @@
     for k in range(GROUPS - 1):
         peer = (here + k + 1) % GROUPS
         along_pts(centers.at[here], centers.at[here], c_send.at[1], c_recv.at[1], peer).start()
-    norms_of(steps // 2, steps)
+    norms_of(steps // 4, steps)
     pb1[...] = jnp.zeros_like(pb1)
     along_pts(rows_in, rows_in, c_send.at[1], c_recv.at[1], here).wait_recv()
     for g in range(GROUPS):
@@ -386,8 +386,8 @@
         copy4(end - 2).wait_recv()
         second_only((2 * steps - LAG + 2) * HALF, HALF)
         end_send3(0)
+        second_only((2 * steps - LAG + 3) * HALF, HALF)
         end_send3(1)
-        second_only((2 * steps - LAG + 3) * HALF, HALF)
         send4(end - 1)
         copy4(end - 1).wait_recv()
         second_only((2 * steps - LAG + 4) * HALF, HALF)

time: 81.4 us -> 81.4 us (level)
  no operation moved by 1% of the time
where the time goes in v9:
time: 81.4 us; the launch traced here: 81.2 us
  Pallas kernels  79.9 us (98%)
  other arithmetic  1.33 us (2%)
    pallas_call x1, Pallas kernels, per_device(): pl.pallas_call(functools.partial(body, steps), out_shape=jax.ShapeDtypeSt...  79.9 us

profile of v9, /device:TPU:1, one launch (start us, length us, event | category | flops | bytes accessed | tf_op | source)
XLA Modules:
  0.0 81.2 jit_solution(2061208454976241294)
XLA Ops:
  0.0 79.9 %shard_map.37 = f32[32,128]{1,0:T(8,128)} custom-call(s32[1024]{0:T(1024)} %ids.1, bf16[32,1024]{1,0:T(8,128)(2,1)} %bitcast.3, bf16[32768,128]{1,0:T(8,128)(2,1)} %points.1), custom_call_target="tpu_custom_call" | custom-call | tf_op jit(solution)/shard_map/pallas_call | solution.py:446
  79.9 1.3 %multiply_bitcast_fusion = f32[128,32]{0,1:T(8,128)} fusion(f32[32,128]{1,0:T(8,128)} %shard_map.37), kind=kLoop, calls=%fused_computation | loop fusion | flops 4096 | bytes 32768 | tf_op jit(solution)/shard_map/div | solution.py:478

commit v10 on v9

--- a/solution.py
+++ b/solution.py
@@ -86,14 +86,14 @@
             peer = (here + k + 1) % GROUPS
 
             def some(i, carry):
-                for u in range(32):
-                    row_at = i * 32 + u
+                for u in range(64):
+                    row_at = i * 64 + u
                     at = ids[peer * 128 + row_at] - here * slab
                     at = jnp.where((at >= 0) & (at < slab), at, slab)
                     picked_f[pl.ds(row_at, 1), :] = xf[pl.ds(at, 1), :]
                 return carry
 
-            lax.fori_loop(0, 4, some, 0)
+            lax.fori_loop(0, 2, some, 0)
             picked[peer] = picked_f[...].astype(BF16)
 
             @pl.when(k < GROUPS - 1)

time: 81.4 us -> 81.4 us (level)
  no operation moved by 1% of the time
where the time goes in v10:
time: 81.4 us; the launch traced here: 81.2 us
  Pallas kernels  79.9 us (98%)
  other arithmetic  1.33 us (2%)
    pallas_call x1, Pallas kernels, per_device(): pl.pallas_call(functools.partial(body, steps), out_shape=jax.ShapeDtypeSt...  79.9 us

profile of v10, /device:TPU:1, one launch (start us, length us, event | category | flops | bytes accessed | tf_op | source)
XLA Modules:
  0.0 81.2 jit_solution(1197309833695451329)
XLA Ops:
  0.0 79.9 %shard_map.37 = f32[32,128]{1,0:T(8,128)} custom-call(s32[1024]{0:T(1024)} %ids.1, bf16[32,1024]{1,0:T(8,128)(2,1)} %bitcast.3, bf16[32768,128]{1,0:T(8,128)(2,1)} %points.1), custom_call_target="tpu_custom_call" | custom-call | tf_op jit(solution)/shard_map/pallas_call | solution.py:446
  79.9 1.3 %multiply_bitcast_fusion = f32[128,32]{0,1:T(8,128)} fusion(f32[32,128]{1,0:T(8,128)} %shard_map.37), kind=kLoop, calls=%fused_computation | loop fusion | flops 4096 | bytes 32768 | tf_op jit(solution)/shard_map/div | solution.py:478
